TPU v7x, 256 devices: a whole 4x4x8 slice. The times are simulated.
256 devices in a mesh: dp: 16 (over y, x_lo, core), tensor: 16 (over z, x_hi).
Axes of the slice: x: 4 (x_hi: 2, x_lo: 2; x = x_hi * 2 + x_lo), y: 4, z: 8, core: 2. Of those that a mesh axis runs over, the one named last changes fastest.
Arguments:
- in_one: bfloat16 [65536, 5120], P('dp', 'tensor'), may hold values from -6 to 6
- grad_one: bfloat16 [65536, 5120], P('dp', 'tensor'), may hold values from -6 to 6
- in_two: bfloat16 [65536, 5120], P('dp', 'tensor'), may hold values from -6 to 6
- grad_two: bfloat16 [65536, 5120], P('dp', 'tensor'), may hold values from -6 to 6
- proj_in_one: bfloat16 [5120, 64], P('tensor'), may hold values from -0.078125 to 0.078125
- proj_out_one: bfloat16 [5120, 64], P('tensor'), may hold values from -0.078125 to 0.078125
- proj_in_two: bfloat16 [5120, 64], P('tensor'), may hold values from -0.078125 to 0.078125
- proj_out_two: bfloat16 [5120, 64], P('tensor'), may hold values from -0.078125 to 0.078125
- query_index: int32 [64], replicated, may hold values from 0 to 511
Outputs:
- gram: float32 [2, 4096, 4096], P(None, 'tensor', 'dp')
- scores: float32 [64, 512], P('tensor', 'dp')
All inputs are finite; a program needn't handle non-finite values.
Results may differ from a plain program's by a relative error of at most 0.0038.
Values may be sent and summed in bfloat16 or wider, within the bound.
A program may use at most 64 MiB of HBM per device.

v0:
```python
import jax
import jax.numpy as jnp
from jax import lax
from jax.sharding import PartitionSpec as P

SEQ = 128


def local(
    in_one,
    grad_one,
    in_two,
    grad_two,
    proj_in_one,
    proj_out_one,
    proj_in_two,
    proj_out_two,
    query_index,
):
    tok_rows = in_one.shape[0]
    rank = proj_in_one.shape[1]
    examples_dev = tok_rows // SEQ
    tensor_count = lax.axis_size("tensor")
    tensor_place = lax.axis_index("tensor")
    share = rank * rank // tensor_count
    scale_seq = jnp.sqrt(jnp.float32(SEQ))
    partial_proj = jnp.stack(
        [
            jnp.dot(in_one, proj_in_one, preferred_element_type=jnp.float32),
            jnp.dot(grad_one, proj_out_one, preferred_element_type=jnp.float32),
            jnp.dot(in_two, proj_in_two, preferred_element_type=jnp.float32),
            jnp.dot(grad_two, proj_out_two, preferred_element_type=jnp.float32),
        ],
        1,
    )
    summed = lax.psum(partial_proj, "tensor")
    summed = summed.reshape(examples_dev, SEQ, 2, 2, rank)
    outer = jnp.einsum(
        "esla,eslb->elab", summed[:, :, :, 1], summed[:, :, :, 0], precision=lax.Precision.HIGHEST
    )
    full_feat = (outer / scale_seq).reshape(examples_dev, 2, rank * rank).astype(jnp.bfloat16)
    own_feat = lax.dynamic_slice_in_dim(full_feat, tensor_place * share, share, 2)
    dp_count = lax.axis_size("dp")
    examples_all = examples_dev * dp_count
    gram_part = jnp.einsum("eli,elj->lij", own_feat, full_feat, preferred_element_type=jnp.float32)
    gram = lax.psum_scatter(gram_part, "dp", scatter_dimension=2, tiled=True) / examples_all
    own_flat = own_feat.reshape(examples_dev, 2 * share)
    local_index = query_index - lax.axis_index("dp") * examples_dev
    selector = (local_index[:, None] == jnp.arange(examples_dev, dtype=jnp.int32)[None, :]).astype(
        jnp.bfloat16
    )
    picked = jnp.dot(selector, own_flat, preferred_element_type=jnp.float32)
    query_feat = lax.psum(picked.astype(jnp.bfloat16), "dp")
    score_part = lax.dot_general(
        query_feat, own_flat, (((1,), (1,)), ((), ())), preferred_element_type=jnp.float32
    )
    scores = lax.psum_scatter(score_part, "tensor", scatter_dimension=0, tiled=True)
    scores = scores / jnp.sqrt(jnp.float32(2 * rank * rank))
    return (gram, scores)


def solution(mesh):
    in_specs = (
        P("dp", "tensor"),
        P("dp", "tensor"),
        P("dp", "tensor"),
        P("dp", "tensor"),
        P("tensor", None),
        P("tensor", None),
        P("tensor", None),
        P("tensor", None),
        P(),
    )
    out_specs = (P(None, "tensor", "dp"), P("tensor", "dp"))
    return jax.shard_map(local, mesh=mesh, in_specs=in_specs, out_specs=out_specs, check_vma=False)
```

profile of v0, /device:TPU:1, one launch (start us, length us, event | category | flops | bytes accessed | tf_op | source)
XLA Modules:
  0.0 464.4 jit_solution(13682627127516252939)
XLA Ops:
  7.2 1.7 copy-done
  8.9 1.6 convolution_bitcast_fusion.3
  10.7 0.6 convolution_bitcast_fusion.2
  11.3 1.1 copy-done.2
  12.4 0.6 convolution_bitcast_fusion.1
  13.1 1.1 copy-done.3
  14.2 0.6 convolution_bitcast_fusion
  15.3 0.8 copy.23
  16.0 4.4 copy.18
  20.5 0.6 copy-done.7
  21.1 207.8 %all-reduce.4.cloned.1.call-done = f32[32,128,2,2,64]{1,4,2,0,3:T(8,128)} async-done(((f32[32,128,2,2,64]{1,4,2,0,3:T(8,128)}), f32[32,128,2,2,64]{1,4,2,0,3:T(8,128)}) %all-reduce.4.cloned.1.call-update) | async-done | bytes 4194320 | tf_op jit(solution)/shard_map/psum | solution.py:36
  228.8 6.6 %multiply_convert_fusion = bf16[32,2,64,64]{3,2,1,0:T(8,128)(2,1)} fusion(f32[32,128,2,2,64]{1,4,2,0,3:T(8,128)} %all-reduce.4.cloned.1.call-done), kind=kOutput, calls=%fused_computation.8 | convolution fusion | flops 403177472 | bytes 4718592 | tf_op jit(solution)/shard_map/esla,eslb->elab/dot_general | solution.py:38
  235.4 3.0 convert_element_type.11
  238.4 1.3 copy.19
  239.8 0.8 convolution_convert_fusion
  240.7 4.5 fusion.1
  245.3 0.6 copy-done.8
  245.9 0.6 dynamic-slice
  247.1 105.1 %all-reduce.6.cloned.1.call-done = bf16[64,512]{1,0:T(8,128)(2,1)} async-done(((bf16[64,512]{1,0:T(8,128)(2,1)}), bf16[64,512]{1,0:T(8,128)(2,1)}) %all-reduce.6.cloned.1.call-update) | async-done | bytes 65552 | tf_op jit(solution)/shard_map/psum | solution.py:53
  352.3 1.0 fusion.5
  353.2 64.5 %all-reduce = f32[64,32]{1,0:T(8,128)S(1)} all-reduce(f32[64,32]{1,0:T(8,128)S(1)} %fusion.5), channel_id=3, replica_groups=mesh['dp'=16,'tensor'=16] {'tensor'}, use_global_device_ids=true, to_apply=%region_3.0.clone | all-reduce | flops 2048 | bytes 16384
  417.8 0.6 dynamic-slice_multiply_fusion
  418.3 37.6 %reduce-scatter.2.cloned.1.call-done = f32[2,256,256]{2,1,0:T(8,128)} async-done(((f32[2,256,4096]{2,1,0:T(8,128)}), f32[2,256,256]{2,1,0:T(8,128)}) %reduce-scatter.2.cloned.1.call-update) | async-done | bytes 524304 | tf_op jit(solution)/shard_map/reduce_scatter | solution.py:46
  456.0 1.9 broadcast_multiply_fusion
  (23 shorter events, 0.8 us)
Async XLA Ops:
  7.2 1.7 copy-start
  7.2 3.3 copy-start.4
  7.2 221.6 %all-reduce.4.cloned.1.call-start = ((), (), s32[]{:S(2)}) async-start(), calls=%async_computation.1 | async-start | bytes 8388608 | tf_op jit(solution)/shard_map/psum | solution.py:36
  8.9 1.8 copy-start.1
  10.7 1.7 copy-start.2
  10.7 1.7 copy-start.5
  12.4 1.7 copy-start.3
  12.4 1.7 copy-start.6
  20.4 0.7 copy-start.7
  20.4 331.8 %all-reduce.6.cloned.1.call-start = ((), (), s32[]{:S(2)}) async-start(), calls=%async_computation.3 | async-start | bytes 131072 | tf_op jit(solution)/shard_map/psum | solution.py:53
  240.7 215.3 %reduce-scatter.2.cloned.1.call-start = ((), (), s32[]{:S(2)}) async-start(), calls=%async_computation.2 | async-start | bytes 8912896 | tf_op jit(solution)/shard_map/reduce_scatter | solution.py:46
  245.2 0.7 copy-start.8
Sparse Core Ops, SparseCore 0:
  20.6 208.2 all-reduce.3
  240.8 111.4 all-reduce.5
  355.0 100.9 reduce-scatter.1
where the time goes:
time: 465 us; the launch traced here: 464 us
  waiting for transfers between devices  351 us (75%)
  blocking collectives  64.5 us (14%)
  matrix products  16.4 us (4%)
  local copies, waits for them, and re-layouts  15.4 us (3%)
  between operations  14.5 us (3%)
    psum x1, waiting for transfers between devices, local(): summed = lax.psum(partial_proj, 'tensor')  208 us
    psum x1, waiting for transfers between devices, local(): query_feat = lax.psum(picked.astype(jnp.bfloat16), 'dp')  105 us
    unnamed x1, blocking collectives  64.5 us
    reduce_scatter x1, waiting for transfers between devices, local(): lax.psum_scatter(gram_part, 'dp', scatter_dimension=2, tiled=True)  37.6 us
  transfers between devices with their start and end apart: 3, of which 3 were waited for; matrix products, arithmetic and copies ran while one was open for 1% of the time, Pallas kernels for 0%

commit v1 on v0

--- a/solution.py
+++ b/solution.py
@@ -21,10 +21,9 @@
     rank = proj_in_one.shape[1]
     examples_dev = tok_rows // SEQ
     tensor_count = lax.axis_size("tensor")
-    tensor_place = lax.axis_index("tensor")
     share = rank * rank // tensor_count
     scale_seq = jnp.sqrt(jnp.float32(SEQ))
-    partial_proj = jnp.stack(
+    partial_proj = jnp.concatenate(
         [
             jnp.dot(in_one, proj_in_one, preferred_element_type=jnp.float32),
             jnp.dot(grad_one, proj_out_one, preferred_element_type=jnp.float32),
@@ -33,24 +32,29 @@
         ],
         1,
     )
-    summed = lax.psum(partial_proj, "tensor")
-    summed = summed.reshape(examples_dev, SEQ, 2, 2, rank)
+    summed = lax.psum_scatter(partial_proj, "tensor", scatter_dimension=0, tiled=True)
+    mine = examples_dev // tensor_count
+    summed = summed.reshape(mine, SEQ, 2, 2, rank)
     outer = jnp.einsum(
         "esla,eslb->elab", summed[:, :, :, 1], summed[:, :, :, 0], precision=lax.Precision.HIGHEST
     )
-    full_feat = (outer / scale_seq).reshape(examples_dev, 2, rank * rank).astype(jnp.bfloat16)
-    own_feat = lax.dynamic_slice_in_dim(full_feat, tensor_place * share, share, 2)
+    feat = (outer / scale_seq).reshape(mine, 2, rank * rank).astype(jnp.bfloat16)
     dp_count = lax.axis_size("dp")
     examples_all = examples_dev * dp_count
-    gram_part = jnp.einsum("eli,elj->lij", own_feat, full_feat, preferred_element_type=jnp.float32)
-    gram = lax.psum_scatter(gram_part, "dp", scatter_dimension=2, tiled=True) / examples_all
-    own_flat = own_feat.reshape(examples_dev, 2 * share)
-    local_index = query_index - lax.axis_index("dp") * examples_dev
-    selector = (local_index[:, None] == jnp.arange(examples_dev, dtype=jnp.int32)[None, :]).astype(
+    by_tensor = feat.reshape(mine, 2, tensor_count, share)
+    own_feat = lax.all_to_all(by_tensor, "tensor", 2, 0, tiled=True).reshape(examples_dev, 2, share)
+    rows = lax.all_gather(own_feat, "dp", axis=0, tiled=True)
+    share_dp = rank * rank // dp_count
+    by_dp = feat.reshape(mine, 2, dp_count, share_dp)
+    cols = lax.all_to_all(by_dp, "dp", 2, 0, tiled=True).reshape(dp_count, 1, mine, 2, share_dp)
+    cols = lax.all_gather(cols, "tensor", axis=1, tiled=True).reshape(examples_all, 2, share_dp)
+    gram = jnp.einsum("eli,elj->lij", rows, cols, preferred_element_type=jnp.float32) / examples_all
+    flat = rows.reshape(examples_all, 2 * share)
+    selector = (query_index[:, None] == jnp.arange(examples_all, dtype=jnp.int32)[None, :]).astype(
         jnp.bfloat16
     )
-    picked = jnp.dot(selector, own_flat, preferred_element_type=jnp.float32)
-    query_feat = lax.psum(picked.astype(jnp.bfloat16), "dp")
+    query_feat = jnp.dot(selector, flat, preferred_element_type=jnp.float32).astype(jnp.bfloat16)
+    own_flat = own_feat.reshape(examples_dev, 2 * share)
     score_part = lax.dot_general(
         query_feat, own_flat, (((1,), (1,)), ((), ())), preferred_element_type=jnp.float32
     )

time: 465 us -> 401 us (0.86)
  the two profiles are of different devices: /device:TPU:1 before, /device:TPU:2 now
where the time goes in v1:
time: 401 us; the launch traced here: 400 us
  waiting for transfers between devices  218 us (54%)
  blocking collectives  136 us (34%)
  between operations  14.8 us (4%)
  starting transfers between devices  12.5 us (3%)
  local copies, waits for them, and re-layouts  8.62 us (2%)
  matrix products  7.42 us (2%)
    reduce_scatter x1, waiting for transfers between devices, local(): lax.psum_scatter(partial_proj, 'tensor', scatter_dimension=0, tiled=True)  215 us
    unnamed x1, blocking collectives  71.9 us
    all_gather x1, blocking collectives, local(): lax.all_gather(cols, 'tensor', axis=1, tiled=True)  44 us
    all_gather x1, blocking collectives, local(): rows = lax.all_gather(own_feat, 'dp', axis=0, tiled=True)  19.9 us
  transfers between devices with their start and end apart: 3, of which 2 were waited for; matrix products, arithmetic and copies ran while one was open for 0% of the time, Pallas kernels for 0%

profile of v1, /device:TPU:2, one launch (start us, length us, event | category | flops | bytes accessed | tf_op | source)
XLA Modules:
  0.0 400.2 jit_solution(3542078863182964024)
XLA Ops:
  7.2 1.7 copy-done
  8.9 1.6 fusion.5
  10.7 0.6 fusion.6
  11.3 1.1 copy-done.2
  12.4 0.6 fusion.7
  13.1 1.1 copy-done.3
  14.2 0.6 fusion.8
  14.8 2.4 pad_maximum_fusion
  17.3 214.6 %reduce-scatter.2.cloned.1.call-done = f32[256,256]{0,1:T(8,128)} async-done(((f32[4096,256]{0,1:T(8,128)}), f32[256,256]{0,1:T(8,128)}) %reduce-scatter.2.cloned.1.call-update) | async-done | bytes 262160 | tf_op jit(solution)/shard_map/reduce_scatter | solution.py:35
  231.8 1.1 reshape.28
  232.9 0.3 fusion
  233.4 0.6 copy.23
  234.0 5.8 %all-to-all-start.1 = ((bf16[2,2,16,256]{3,1,0,2:T(2,128)(2,1)}), bf16[2,2,16,256]{3,1,0,2:T(2,128)(2,1)S(1)}, u32[]{:S(2)}, u32[]{:S(2)}) async-start(bf16[2,2,16,256]{3,1,0,2:T(2,128)(2,1)} %copy.23), calls=%async_computation.2 | async-start | bytes 65536 | tf_op jit(solution)/shard_map/all_to_all | solution.py:49
  239.8 0.6 dynamic-slice
  241.1 3.6 all-to-all-done.1
  244.6 6.6 %all-to-all-start = ((bf16[2,2,16,256]{3,1,0,2:T(2,128)(2,1)}), bf16[2,2,16,256]{3,1,0,2:T(2,128)(2,1)S(1)}, u32[]{:S(2)}, u32[]{:S(2)}) async-start(bf16[2,2,16,256]{3,1,0,2:T(2,128)(2,1)} %copy.23), calls=%async_computation.1 | async-start | bytes 65536 | tf_op jit(solution)/shard_map/all_to_all | solution.py:45
  251.3 44.0 %all-gather = bf16[16,32,2,1,256]{4,0,3,2,1:T(8,128)(2,1)S(1)} all-gather(bf16[16,2,2,1,256]{4,0,3,2,1:T(8,128)(2,1)S(1)} %copy.26), channel_id=2, replica_groups=mesh['dp'=16,'tensor'=16] {'tensor'}, dimensions={1}, use_global_device_ids=true | all-gather | bytes 557056 | tf_op jit(solution)/shard_map/all_gather | solution.py:50
  295.3 1.1 copy.27
  296.4 19.9 %all_gather.6 = bf16[512,2,256]{2,0,1:T(8,128)(2,1)S(1)} all-gather(bf16[32,2,256]{2,0,1:T(8,128)(2,1)S(1)} %copy.29), channel_id=1, replica_groups=mesh['dp'=16,'tensor'=16] {'dp'}, dimensions={0}, use_global_device_ids=true | all-gather | bytes 557056 | tf_op jit(solution)/shard_map/all_gather | solution.py:46
  316.3 1.0 copy.28
  317.3 1.4 fusion.1
  318.7 71.9 %all-reduce = f32[64,32]{1,0:T(8,128)S(1)} all-reduce(f32[64,32]{1,0:T(8,128)S(1)} %fusion.1), channel_id=4, replica_groups=mesh['dp'=16,'tensor'=16] {'tensor'}, use_global_device_ids=true, to_apply=%region_1.0.clone | all-reduce | flops 2048 | bytes 16384
  390.6 2.2 convolution_multiply_fusion
  392.8 0.6 dynamic-slice_multiply_fusion
  (23 shorter events, 0.4 us)
Async XLA Ops:
  7.2 1.7 copy-start
  7.2 3.3 copy-start.4
  7.2 224.6 %reduce-scatter.2.cloned.1.call-start = ((), (), s32[]{:S(2)}) async-start(), calls=%async_computation.3 | async-start | bytes 4456448 | tf_op jit(solution)/shard_map/reduce_scatter | solution.py:35
  8.9 1.8 copy-start.1
  10.7 1.7 copy-start.2
  10.7 1.7 copy-start.5
  12.4 1.7 copy-start.3
  12.4 1.7 copy-start.6
  17.2 222.6 %copy-start.8 = (u32[256]{0:T(256)S(1)}, u32[256]{0:T(256)}, u32[]{:S(2)}) copy-start(u32[256]{0:T(256)} %constant.11) | copy-start | bytes 3076
  17.2 300.0 %copy-start.7 = (s32[64]{0:T(128)S(1)}, s32[64]{0:T(128)}, u32[]{:S(2)}) copy-start(s32[64]{0:T(128)} %param.17) | copy-start | bytes 772
  234.0 10.6 %all-to-all-start.1 = ((bf16[2,2,16,256]{3,1,0,2:T(2,128)(2,1)}), bf16[2,2,16,256]{3,1,0,2:T(2,128)(2,1)S(1)}, u32[]{:S(2)}, u32[]{:S(2)}) async-start(bf16[2,2,16,256]{3,1,0,2:T(2,128)(2,1)} %copy.23), calls=%async_computation.2 | async-start | bytes 65536 | tf_op jit(solution)/shard_map/all_to_all | solution.py:49
  244.6 51.7 %all-to-all-start = ((bf16[2,2,16,256]{3,1,0,2:T(2,128)(2,1)}), bf16[2,2,16,256]{3,1,0,2:T(2,128)(2,1)S(1)}, u32[]{:S(2)}, u32[]{:S(2)}) async-start(bf16[2,2,16,256]{3,1,0,2:T(2,128)(2,1)} %copy.23), calls=%async_computation.1 | async-start | bytes 65536 | tf_op jit(solution)/shard_map/all_to_all | solution.py:45
Sparse Core Ops, SparseCore 0:
  17.4 214.4 reduce-scatter.1

commit v2 on v0

v2 whole, which is shorter than its diff:
```python
import math

import jax
import jax.numpy as jnp
from jax import lax
from jax.experimental import pallas as pl
from jax.experimental.pallas import tpu as pltpu
from jax.sharding import PartitionSpec as P

SEQ = 128
RANK = 64
GROUP = 16
RING = 8
LANES = 128
PACK = 2 * SEQ + 16
MESH = pl.DeviceIdType.MESH
AWAY = (4, -3, 3, -2, 2, -1, 1, 0)


def encode(dst, layers):
    keys = []
    for which, values in enumerate(layers):
        top = jnp.max(jnp.abs(values), axis=0, keepdims=True)
        key = jnp.ceil(8.0 * jnp.log2(jnp.maximum(top, 1e-30)) + 0.1)
        scaled = jnp.round(values * jnp.exp2(15.0 - key * 0.125))
        dst[which * SEQ : (which + 1) * SEQ, :] = scaled.astype(jnp.int32).astype(jnp.int16)
        keys.append(key)
    row = lax.broadcasted_iota(jnp.int32, (16, LANES), 0)
    both = jnp.where(row < 8, keys[0], keys[1])
    dst[2 * SEQ : PACK, :] = both.astype(jnp.int32).astype(jnp.int16)


def decode(src):
    keys = src[2 * SEQ : PACK, :].astype(jnp.int32).astype(jnp.float32)
    out = []
    for which in range(2):
        step = jnp.exp2(keys[8 * which : 8 * which + 1, :] * 0.125 - 15.0)
        whole = src[which * SEQ : (which + 1) * SEQ, :].astype(jnp.int32).astype(jnp.float32)
        out.append(whole * step)
    return out


def add(one, two):
    return [a + b for a, b in zip(one, two)]


def kernel(
    in_one, grad_one, in_two, grad_two, w_in_one, w_out_one, w_in_two, w_out_two, query,
    gram, scores,
    tok, wide, part, a_out, a_got, b_out, b_got, x_out, x_got, square, slices, land_t, land_d,
    rows, cols, swap, pick, turned, score_out, score_got,
    in_sem, a_ss, a_rs, b_ss, b_rs, x_ss, x_rs, lt_ss, lt_rs, ld_ss, ld_rs,
    t_ss, t_rs, d_ss, d_rs, dx_ss, dx_rs, s_ss, s_rs,
):
    d = lax.axis_index("dp")
    t = lax.axis_index("tensor")
    z, xh = t // 2, t % 2
    way = 1 - 2 * (d % 2)
    owners = [lax.rem(z + way * step + RING, RING) for step in AWAY]
    forward = (d, lax.rem(z + way + RING, RING) * 2 + xh)
    backward = (d, lax.rem(z - way + RING, RING) * 2 + xh)
    partner = (d, z * 2 + 1 - xh)
    sends = []

    def send(src, dst, ss, rs, device):
        copy = pltpu.make_async_remote_copy(
            src_ref=src, dst_ref=dst, send_sem=ss, recv_sem=rs, device_id=device, device_id_type=MESH
        )
        copy.start()
        sends.append(copy)

    def landed(ref, rs):
        pltpu.make_async_copy(ref, ref, rs).wait()

    loads = {}
    for i in range(RING):
        for half in range(2):
            start = pl.multiple_of((half * GROUP + 2 * owners[i]) * SEQ, 2 * SEQ)
            for k, source in enumerate((in_one, grad_one, in_two, grad_two)):
                copy = pltpu.make_async_copy(
                    source.at[pl.ds(start, 2 * SEQ)],
                    tok.at[k, pl.ds(start, 2 * SEQ)],
                    in_sem.at[i, half, k],
                )
                copy.start()
                loads[i, half, k] = copy

    barrier = pltpu.get_barrier_semaphore()
    for k in range(1, GROUP):
        pl.semaphore_signal(
            barrier, inc=1, device_id=(d, lax.rem(t + k, GROUP)), device_id_type=MESH
        )
        pl.semaphore_signal(
            barrier, inc=1, device_id=(lax.rem(d + k, GROUP), t), device_id_type=MESH
        )

    blank = jnp.zeros((w_in_one.shape[0], RANK), jnp.bfloat16)
    for k, weight in enumerate((w_in_one, w_out_one, w_in_two, w_out_two)):
        sides = [weight[...], blank] if k % 2 == 0 else [blank, weight[...]]
        wide[k] = jnp.concatenate(sides, 1)

    def project(i, half):
        first = half * GROUP + 2 * owners[i]
        start = pl.multiple_of(first * SEQ, 2 * SEQ)
        for k in range(4):
            loads[i, half, k].wait()
        for layer in range(2):
            both = jnp.dot(
                tok[2 * layer, pl.ds(start, 2 * SEQ), :],
                wide[2 * layer],
                preferred_element_type=jnp.float32,
            ) + jnp.dot(
                tok[2 * layer + 1, pl.ds(start, 2 * SEQ), :],
                wide[2 * layer + 1],
                preferred_element_type=jnp.float32,
            )
            part[first, layer] = both[:SEQ]
            part[first + 1, layer] = both[SEQ:]

    def own(half, owner, side):
        index = half * GROUP + 2 * owner + side
        return [part[index, 0], part[index, 1]]

    def ring_a(i):
        for side in range(2):
            total = own(0, owners[i], side)
            if i >= 2:
                landed(a_got.at[i - 2, side], a_rs.at[i - 2, side])
                total = add(total, decode(a_got.at[i - 2, side]))
            encode(a_out.at[i, side], total)
            send(
                a_out.at[i, side], a_got.at[i, side], a_ss.at[i, side], a_rs.at[i, side],
                forward if i % 2 == 0 else backward,
            )

    def pair(i):
        encode(x_out.at[i], own(1, owners[i], 1 - xh))
        send(x_out.at[i], x_got.at[i], x_ss.at[i], x_rs.at[i], partner)

    def ring_b(i):
        landed(x_got.at[i], x_rs.at[i])
        total = add(own(1, owners[i], xh), decode(x_got.at[i]))
        if i >= 2:
            landed(b_got.at[i - 2], b_rs.at[i - 2])
            total = add(total, decode(b_got.at[i - 2]))
        encode(b_out.at[i], total)
        send(
            b_out.at[i], b_got.at[i], b_ss.at[i], b_rs.at[i], forward if i % 2 == 0 else backward
        )

    for i in range(RING + 1):
        if i < RING:
            project(i, 0)
            if i == 0:
                pl.semaphore_wait(barrier, 2 * (GROUP - 1))
            if i < RING - 1:
                ring_a(i)
            project(i, 1)
            pair(i)
        if i >= 2:
            ring_b(i - 2)

    for side in range(2):
        for i in (5, 6):
            landed(a_got.at[i, side], a_rs.at[i, side])

    def over_z(side):
        total = own(0, z, side)
        for i in (5, 6):
            total = add(total, decode(a_got.at[i, side]))
        return total

    encode(x_out.at[RING], over_z(1 - xh))
    send(x_out.at[RING], x_got.at[RING], x_ss.at[RING], x_rs.at[RING], partner)

    at_row = lax.broadcasted_iota(jnp.int32, (GROUP * 32, GROUP * 32), 0)
    at_col = lax.broadcasted_iota(jnp.int32, (GROUP * 32, GROUP * 32), 1)
    mirrored = (at_row % 16) * 32 + (at_row // 16 % 2) * 16 + at_row // 32
    swap[...] = jnp.where(at_col == mirrored, 1.0, 0.0).astype(jnp.bfloat16)
    example = lax.broadcasted_iota(jnp.int32, pick.shape, 0)
    pick[...] = jnp.where(example == query[...], 1.0, 0.0).astype(jnp.bfloat16)
    score_out[...] = jnp.zeros_like(score_out)

    def features(half, sums):
        for layer in range(2):
            outer = lax.dot_general(
                sums[layer], sums[layer], (((0,), (0,)), ((), ())),
                precision=lax.Precision.HIGHEST, preferred_element_type=jnp.float32,
            )
            scaled = outer[RANK:, :] / jnp.float32(math.sqrt(SEQ))
            square[...] = scaled.astype(jnp.bfloat16).astype(jnp.float32)
            for pair_of in range(2):
                even = square[pl.ds(2 * pair_of, GROUP, stride=4), :]
                odd = square[pl.ds(2 * pair_of + 1, GROUP, stride=4), :]
                slices[pl.ds(half * 4 + layer * 2 + pair_of, GROUP, stride=8), :] = jnp.concatenate(
                    [even[:, :RANK], odd[:, :RANK]], 1
                )

    for i in (5, 6):
        landed(b_got.at[i], b_rs.at[i])
    landed(x_got.at[RING - 1], x_rs.at[RING - 1])
    total = add(own(1, z, xh), decode(x_got.at[RING - 1]))
    for i in (5, 6):
        total = add(total, decode(b_got.at[i]))
    features(1, total)
    landed(x_got.at[RING], x_rs.at[RING])
    features(0, add(over_z(xh), decode(x_got.at[RING])))

    def tile(index):
        return pl.ds(pl.multiple_of(8 * index, 8), 8)

    for k in range(1, GROUP):
        to = lax.rem(t + k, GROUP)
        send(slices.at[tile(to)], land_t.at[tile(t)], lt_ss.at[k], lt_rs.at[k], (d, to))
        to = lax.rem(d + k, GROUP)
        send(slices.at[tile(to)], land_d.at[tile(d)], ld_ss.at[k], ld_rs.at[k], (to, t))
    land_t[tile(t), :] = slices[tile(t), :]
    land_d[tile(d), :] = slices[tile(d), :]

    def gather(land, block, rs):
        for k in range(1, GROUP):
            landed(land.at[pl.ds(0, 8)], rs.at[k])
        for half in range(2):
            lanes = [land[pl.ds(half * 4 + k, GROUP, stride=8), :] for k in range(4)]
            block[half * GROUP : (half + 1) * GROUP, :] = jnp.concatenate(lanes, 1).astype(
                jnp.bfloat16
            )

    def pass_on(step, stream, go):
        side = xh if stream == 0 else 1 - xh
        sign = -way if go == 0 else way
        block = lax.rem(z + sign * step + RING, RING) * 2 + side
        i = 2 * step + go
        send(
            cols.at[block], cols.at[block], d_ss.at[i, stream], d_rs.at[i, stream],
            forward if go == 0 else backward,
        )

    gather(land_d, cols.at[t], ld_rs)
    send(cols.at[t], cols.at[t], dx_ss.at[0], dx_rs.at[0], partner)
    pass_on(0, 0, 0)
    pass_on(0, 0, 1)
    gather(land_t, rows.at[d], lt_rs)
    for k in range(1, GROUP):
        send(rows.at[d], rows.at[d], t_ss.at[k], t_rs.at[k], (lax.rem(d + k, GROUP), t))
    for step in range(4):
        for stream in range(2):
            if step == 0 and stream == 0:
                continue
            for go in range(2):
                if step == 3 and go == 1:
                    continue
                if step == 0:
                    if go == 0:
                        landed(cols.at[0], dx_rs.at[0])
                else:
                    landed(cols.at[0], d_rs.at[2 * (step - 1) + go, stream])
                pass_on(step, stream, go)

    for k in range(1, GROUP):
        landed(rows.at[0], t_rs.at[k])
    mine = rows[d]
    all_rows = rows[...].reshape(GROUP * 32, 4 * LANES)
    query_feat = lax.dot_general(
        pick[...], all_rows, (((0,), (0,)), ((), ())), preferred_element_type=jnp.float32
    ).astype(jnp.bfloat16)
    partial_scores = lax.dot_general(
        query_feat, mine, (((1,), (1,)), ((), ())), preferred_element_type=jnp.float32
    )
    for k in range(GROUP):
        score_out[8 * k : 8 * k + 4, 0:32] = partial_scores[4 * k : 4 * k + 4, :]
    for k in range(1, GROUP):
        to = lax.rem(t + k, GROUP)
        send(score_out.at[tile(to)], score_got.at[tile(t)], s_ss.at[k], s_rs.at[k], (d, to))
    score_got[tile(t), :] = score_out[tile(t), :]
    turned[...] = lax.dot_general(
        all_rows, swap[...], (((0,), (0,)), ((), ())), preferred_element_type=jnp.float32
    ).astype(jnp.bfloat16)

    for stream in range(2):
        for i in (4, 5, 6):
            if i != 4:
                landed(cols.at[0], d_rs.at[i, stream])
    all_cols = cols[...].reshape(GROUP * 32, 4 * LANES)
    for layer in range(2):
        span = slice(layer * 2 * LANES, (layer + 1) * 2 * LANES)
        gram[layer] = jnp.dot(
            turned[span, :], all_cols[:, span], preferred_element_type=jnp.float32
        ) * jnp.float32(1.0 / 512)

    for k in range(1, GROUP):
        landed(score_got.at[pl.ds(0, 8)], s_rs.at[k])
    total = score_got[0:8, :]
    for k in range(1, GROUP):
        total = total + score_got[8 * k : 8 * k + 8, :]
    scores[...] = total[0:4, 0:32] / jnp.float32(math.sqrt(2 * RANK * RANK))
    for copy in sends:
        copy.wait_send()


def local(*args):
    tokens, width = args[0].shape
    query = args[-1].reshape(1, -1)
    dma = pltpu.SemaphoreType.DMA
    f32, bf16, i16 = jnp.float32, jnp.bfloat16, jnp.int16
    vmem = pltpu.VMEM
    scratch = [
        vmem((4, tokens, width), bf16),
        vmem((4, width, LANES), bf16),
        vmem((tokens // SEQ, 2, SEQ, LANES), f32),
        vmem((7, 2, PACK, LANES), i16),
        vmem((7, 2, PACK, LANES), i16),
        vmem((7, PACK, LANES), i16),
        vmem((7, PACK, LANES), i16),
        vmem((RING + 1, PACK, LANES), i16),
        vmem((RING + 1, PACK, LANES), i16),
        vmem((RANK, LANES), f32),
        vmem((8 * GROUP, LANES), f32),
        vmem((8 * GROUP, LANES), f32),
        vmem((8 * GROUP, LANES), f32),
        vmem((GROUP, 32, 4 * LANES), bf16),
        vmem((GROUP, 32, 4 * LANES), bf16),
        vmem((GROUP * 32, GROUP * 32), bf16),
        vmem((GROUP * 32, query.shape[1]), bf16),
        vmem((4 * LANES, GROUP * 32), bf16),
        vmem((8 * GROUP, LANES), f32),
        vmem((8 * GROUP, LANES), f32),
        dma((RING, 2, 4)),
        dma((7, 2)), dma((7, 2)),
        dma((7,)), dma((7,)),
        dma((RING + 1,)), dma((RING + 1,)),
        dma((GROUP,)), dma((GROUP,)),
        dma((GROUP,)), dma((GROUP,)),
        dma((GROUP,)), dma((GROUP,)),
        dma((7, 2)), dma((7, 2)),
        dma((1,)), dma((1,)),
        dma((GROUP,)), dma((GROUP,)),
    ]
    anywhere = pl.BlockSpec(memory_space=pl.ANY)
    in_vmem = pl.BlockSpec(memory_space=pltpu.VMEM)
    return pl.pallas_call(
        kernel,
        out_shape=(
            jax.ShapeDtypeStruct((2, 256, 256), f32),
            jax.ShapeDtypeStruct((4, 32), f32),
        ),
        in_specs=[anywhere] * 4 + [in_vmem] * 5,
        out_specs=(in_vmem, in_vmem),
        scratch_shapes=scratch,
        compiler_params=pltpu.CompilerParams(
            collective_id=0, has_side_effects=True, vmem_limit_bytes=48 << 20
        ),
    )(*args[:-1], query)


def solution(mesh):
    in_specs = (
        P("dp", "tensor"),
        P("dp", "tensor"),
        P("dp", "tensor"),
        P("dp", "tensor"),
        P("tensor", None),
        P("tensor", None),
        P("tensor", None),
        P("tensor", None),
        P(),
    )
    out_specs = (P(None, "tensor", "dp"), P("tensor", "dp"))
    return jax.shard_map(local, mesh=mesh, in_specs=in_specs, out_specs=out_specs, check_vma=False)
```

time: 465 us -> 88.9 us (0.19)
  the two profiles are of different devices: /device:TPU:1 before, /device:TPU:2 now
where the time goes in v2:
time: 88.9 us; the launch traced here: 88.4 us
  Pallas kernels  65.6 us (74%)
  local copies, waits for them, and re-layouts  22.1 us (25%)
    pallas_call x1, Pallas kernels, local(): pl.pallas_call(kernel, out_shape=(jax.ShapeDtypeStruct((2, 256, 256), f32...  65.6 us
    unnamed x12, local copies, waits for them, and re-layouts  22.1 us

profile of v2, /device:TPU:2, one launch (start us, length us, event | category | flops | bytes accessed | tf_op | source)
XLA Modules:
  0.0 88.4 jit_solution(13550034646402920)
XLA Ops:
  0.6 0.9 %copy.15.w_in_one = bf16[320,64]{1,0:T(8,128)(2,1)S(1)} copy(bf16[320,64]{0,1:T(8,128)(2,1)} %param.13) | data formatting | bytes 81920 | tf_op args[4]
  1.5 0.9 %copy.16.w_out_one = bf16[320,64]{1,0:T(8,128)(2,1)S(1)} copy(bf16[320,64]{0,1:T(8,128)(2,1)} %param.14) | data formatting | bytes 81920 | tf_op args[5]
  2.5 0.9 %copy.17.w_in_two = bf16[320,64]{1,0:T(8,128)(2,1)S(1)} copy(bf16[320,64]{0,1:T(8,128)(2,1)} %param.15) | data formatting | bytes 81920 | tf_op args[6]
  3.4 0.9 %copy.18.w_out_two = bf16[320,64]{1,0:T(8,128)(2,1)S(1)} copy(bf16[320,64]{0,1:T(8,128)(2,1)} %param.16) | data formatting | bytes 81920 | tf_op args[7]
  4.3 3.3 %copy.11.in_one = bf16[4096,320]{1,0:T(8,128)(2,1)S(1)} copy(bf16[4096,320]{0,1:T(8,128)(2,1)} %param.9) | data formatting | bytes 5242880 | tf_op args[0]
  7.6 4.5 %copy.12.grad_one = bf16[4096,320]{1,0:T(8,128)(2,1)} copy(bf16[4096,320]{0,1:T(8,128)(2,1)} %param.10) | data formatting | bytes 5242880 | tf_op args[1]
  12.2 4.6 %copy.13.in_two = bf16[4096,320]{1,0:T(8,128)(2,1)} copy(bf16[4096,320]{0,1:T(8,128)(2,1)} %param.11) | data formatting | bytes 5242880 | tf_op args[2]
  16.7 0.0 copy-start
  16.7 4.6 %copy.14.grad_two = bf16[4096,320]{1,0:T(8,128)(2,1)} copy(bf16[4096,320]{0,1:T(8,128)(2,1)} %param.12) | data formatting | bytes 5242880 | tf_op args[3]
  21.4 0.0 copy-done
  21.4 65.6 %shard_map.104 = (f32[2,256,256]{2,1,0:T(8,128)S(1)}, f32[4,32]{1,0:T(4,128)S(1)}) custom-call(bf16[4096,320]{1,0:T(8,128)(2,1)S(1)} %copy.11.in_one, bf16[4096,320]{1,0:T(8,128)(2,1)} %copy.12.grad_one, bf16[4096,320]{1,0:T(8,128)(2,1)} %copy.13.in_two, bf16[4096,320]{1,0:T(8,128)(2,1)} %copy.14.grad_two, bf16[320,64]{1,0:T(8,128)(2,1)S(1)} %copy.15.w_in_one, ...), custom_call_target="tpu_custom_call" | custom-call | tf_op jit(solution)/shard_map/pallas_call | solution.py:341
  87.0 0.8 copy.21
  87.8 0.6 copy.22
Async XLA Ops:
  16.7 4.6 %copy-start = (s32[64]{0:T(128)S(1)}, s32[64]{0:T(128)}, u32[]{:S(2)}) copy-start(s32[64]{0:T(128)} %param.17) | copy-start | bytes 772

commit v3 on v2

v3 whole, which is shorter than its diff:
```python
import math

import jax
import jax.numpy as jnp
from jax import lax
from jax.experimental import pallas as pl
from jax.experimental.pallas import tpu as pltpu
from jax.sharding import PartitionSpec as P

SEQ = 128
RANK = 64
GROUP = 16
RING = 8
LANES = 128
PACK = 4 * RANK + 16
MESH = pl.DeviceIdType.MESH
AWAY = (4, -3, 3, -2, 2, -1, 1, 0)


def encode(dst, layers):
    keys = []
    for which, values in enumerate(layers):
        for side in range(2):
            some = values[side * RANK : (side + 1) * RANK]
            top = jnp.max(jnp.abs(some), axis=0, keepdims=True)
            key = jnp.ceil(8.0 * jnp.log2(jnp.maximum(top, 1e-30)) + 0.1)
            scaled = jnp.round(some * jnp.exp2(15.0 - key * 0.125))
            start = (2 * which + side) * RANK
            dst[start : start + RANK, :] = scaled.astype(jnp.int32).astype(jnp.int16)
            keys.append(key)
    row = lax.broadcasted_iota(jnp.int32, (16, SEQ), 0)
    both = jnp.where(row < 4, keys[0], keys[1])
    both = jnp.where(row < 8, both, jnp.where(row < 12, keys[2], keys[3]))
    dst[4 * RANK : PACK, :] = both.astype(jnp.int32).astype(jnp.int16)


def decode(src):
    keys = src[4 * RANK : PACK, :].astype(jnp.int32).astype(jnp.float32)
    out = []
    for which in range(4):
        step = jnp.exp2(keys[4 * which : 4 * which + 1, :] * 0.125 - 15.0)
        whole = src[which * RANK : (which + 1) * RANK, :].astype(jnp.int32).astype(jnp.float32)
        out.append(whole * step)
    return [jnp.concatenate(out[:2], 0), jnp.concatenate(out[2:], 0)]


def add(one, two):
    return [a + b for a, b in zip(one, two)]


def kernel(
    in_one, grad_one, in_two, grad_two, w_in_one, w_out_one, w_in_two, w_out_two, asked,
    gram, scores,
    tok, weights, query, part, a_out, a_got, b_out, b_got, x_out, x_got, square, slices, land_t, land_d,
    rows, cols, swap, pick, turned, score_out, score_got,
    in_sem, w_sem, q_sem, a_ss, a_rs, b_ss, b_rs, x_ss, x_rs, lt_ss, lt_rs, ld_ss, ld_rs,
    t_ss, t_rs, d_ss, d_rs, s_ss, s_rs,
):
    d = lax.axis_index("dp")
    t = lax.axis_index("tensor")
    z, xh = t // 2, t % 2
    way = 1 - 2 * (d % 2)
    owners = [lax.rem(z + way * step + RING, RING) for step in AWAY]
    forward = (d, lax.rem(z + way + RING, RING) * 2 + xh)
    backward = (d, lax.rem(z - way + RING, RING) * 2 + xh)
    partner = (d, z * 2 + 1 - xh)
    def send(src, dst, ss, rs, device):
        pltpu.make_async_remote_copy(
            src_ref=src, dst_ref=dst, send_sem=ss, recv_sem=rs, device_id=device, device_id_type=MESH
        ).start()

    def landed(ref, sem):
        pltpu.make_async_copy(ref, ref, sem).wait()

    barrier = pltpu.get_barrier_semaphore()
    for k in range(1, GROUP):
        pl.semaphore_signal(
            barrier, inc=1, device_id=(d, lax.rem(t + k, GROUP)), device_id_type=MESH
        )
        pl.semaphore_signal(
            barrier, inc=1, device_id=(lax.rem(d + k, GROUP), t), device_id_type=MESH
        )

    def load(i):
        for half in range(2):
            start = pl.multiple_of((half * GROUP + 2 * owners[i]) * SEQ, 2 * SEQ)
            for k, source in enumerate((in_one, grad_one, in_two, grad_two)):
                pltpu.make_async_copy(
                    source.at[:, pl.ds(start, 2 * SEQ)],
                    tok.at[k, :, pl.ds(start, 2 * SEQ)],
                    in_sem.at[i, half],
                ).start()

    for k, weight in enumerate((w_in_one, w_out_one, w_in_two, w_out_two)):
        pltpu.make_async_copy(weight, weights.at[k], w_sem.at[0]).start()
    for i in range(3):
        load(i)
    pltpu.make_async_copy(asked, query, q_sem.at[0]).start()
    landed(weights, w_sem.at[0])

    def project(i, half):
        first = half * GROUP + 2 * owners[i]
        start = pl.multiple_of(first * SEQ, 2 * SEQ)
        landed(tok.at[:, :, pl.ds(start, 2 * SEQ)], in_sem.at[i, half])
        for k in range(4):
            both = jnp.dot(
                weights[k],
                tok[k, :, pl.ds(start, 2 * SEQ)],
                preferred_element_type=jnp.float32,
            )
            span = slice(k % 2 * RANK, (k % 2 + 1) * RANK)
            part[first, k // 2, span, :] = both[:, :SEQ]
            part[first + 1, k // 2, span, :] = both[:, SEQ:]

    def own(half, owner, side):
        index = half * GROUP + 2 * owner + side
        return [part[index, 0], part[index, 1]]

    def ring_a(i):
        for side in range(2):
            total = own(0, owners[i], side)
            if i >= 2:
                landed(a_got.at[i - 2, side], a_rs.at[i - 2, side])
                total = add(total, decode(a_got.at[i - 2, side]))
            encode(a_out.at[i, side], total)
            send(
                a_out.at[i, side], a_got.at[i, side], a_ss.at[0], a_rs.at[i, side],
                forward if i % 2 == 0 else backward,
            )

    def pair(i):
        encode(x_out.at[i], own(1, owners[i], 1 - xh))
        send(x_out.at[i], x_got.at[i], x_ss.at[0], x_rs.at[i], partner)

    def ring_b(i):
        landed(x_got.at[i], x_rs.at[i])
        total = add(own(1, owners[i], xh), decode(x_got.at[i]))
        if i >= 2:
            landed(b_got.at[i - 2], b_rs.at[i - 2])
            total = add(total, decode(b_got.at[i - 2]))
        encode(b_out.at[i], total)
        send(
            b_out.at[i], b_got.at[i], b_ss.at[0], b_rs.at[i], forward if i % 2 == 0 else backward
        )

    for i in range(RING + 1):
        if i < RING:
            project(i, 0)
            if i + 3 < RING:
                load(i + 3)
            if i == 0:
                pl.semaphore_wait(barrier, 2 * (GROUP - 1))
            if i < RING - 1:
                ring_a(i)
            project(i, 1)
            pair(i)
        if i >= 2:
            ring_b(i - 2)

    for side in range(2):
        for i in (5, 6):
            landed(a_got.at[i, side], a_rs.at[i, side])

    def over_z(side):
        total = own(0, z, side)
        for i in (5, 6):
            total = add(total, decode(a_got.at[i, side]))
        return total

    encode(x_out.at[RING], over_z(1 - xh))
    send(x_out.at[RING], x_got.at[RING], x_ss.at[0], x_rs.at[RING], partner)

    at_row = lax.broadcasted_iota(jnp.int32, (GROUP * 32, GROUP * 32), 0)
    at_col = lax.broadcasted_iota(jnp.int32, (GROUP * 32, GROUP * 32), 1)
    mirrored = (at_row % 16) * 32 + (at_row // 16 % 2) * 16 + at_row // 32
    swap[...] = jnp.where(at_col == mirrored, 1.0, 0.0).astype(jnp.bfloat16)
    landed(query, q_sem.at[0])
    row = lax.broadcasted_iota(jnp.int32, pick.shape, 0)
    example = (row // 32 % 8 * 2 + row // 256) * 32 + row % 32
    pick[...] = jnp.where(example == query[...], 1.0, 0.0).astype(jnp.bfloat16)
    score_out[...] = jnp.zeros_like(score_out)

    def features(half, sums):
        for layer in range(2):
            outer = lax.dot_general(
                sums[layer], sums[layer], (((1,), (1,)), ((), ())),
                precision=lax.Precision.HIGHEST, preferred_element_type=jnp.float32,
            )
            scaled = outer[RANK:, :] / jnp.float32(math.sqrt(SEQ))
            square[...] = scaled.astype(jnp.bfloat16).astype(jnp.float32)
            for pair_of in range(2):
                even = square[pl.ds(2 * pair_of, GROUP, stride=4), :]
                odd = square[pl.ds(2 * pair_of + 1, GROUP, stride=4), :]
                slices[pl.ds(half * 4 + layer * 2 + pair_of, GROUP, stride=8), :] = jnp.concatenate(
                    [even[:, :RANK], odd[:, :RANK]], 1
                )

    for i in (5, 6):
        landed(b_got.at[i], b_rs.at[i])
    landed(x_got.at[RING - 1], x_rs.at[RING - 1])
    total = add(own(1, z, xh), decode(x_got.at[RING - 1]))
    for i in (5, 6):
        total = add(total, decode(b_got.at[i]))
    features(1, total)
    landed(x_got.at[RING], x_rs.at[RING])
    features(0, add(over_z(xh), decode(x_got.at[RING])))

    place = d % 2 * 8 + d // 2

    def along(steps):
        return lax.rem(z + steps + RING, RING)

    def tile(index):
        return pl.ds(pl.multiple_of(8 * index, 8), 8)

    for k in range(1, GROUP):
        to = lax.rem(t + k, GROUP)
        send(slices.at[tile(to)], land_t.at[tile(t)], lt_ss.at[0], lt_rs.at[0], (d, to))
    for k in range(1, GROUP):
        to = lax.rem(d + k, GROUP)
        send(slices.at[tile(to)], land_d.at[tile(place)], ld_ss.at[0], ld_rs.at[0], (to, t))
    land_t[tile(t), :] = slices[tile(t), :]
    land_d[tile(place), :] = slices[tile(d), :]

    def gather(land, block, rs):
        landed(land.at[pl.ds(0, 8 * (GROUP - 1))], rs.at[0])
        for half in range(2):
            lanes = [land[pl.ds(half * 4 + k, GROUP, stride=8), :] for k in range(4)]
            block[half * GROUP : (half + 1) * GROUP, :] = jnp.concatenate(lanes, 1).astype(
                jnp.bfloat16
            )

    gather(land_t, rows.at[place], lt_rs)
    for k in range(1, 8):
        send(rows.at[place], rows.at[place], t_ss.at[0], t_rs.at[0], (lax.rem(d + 2 * k, GROUP), t))

    gather(land_d, cols.at[t], ld_rs)
    for i, steps in enumerate((2, -2, 1, -1, 0)):
        for flip in range(2):
            if steps or flip:
                to = along(steps) * 2 + (1 - xh if flip else xh)
                send(cols.at[t], cols.at[t], d_ss.at[0], d_rs.at[0 if i < 2 else 1], (d, to))

    landed(rows.at[pl.ds(0, 7)], t_rs.at[0])
    block = pl.ds(d % 2 * 8, 8)
    sibling = (d + 1 - 2 * (d % 2), t)
    send(rows.at[block], rows.at[block], t_ss.at[1], t_rs.at[1], sibling)

    landed(cols.at[pl.ds(0, 4)], d_rs.at[0])
    for held, steps in ((-2 * way, way), (-2 * way, 2 * way), (2 * way, -way)):
        block = pl.ds(2 * along(held), 2)
        to = along(steps) * 2 + xh
        send(cols.at[block], cols.at[block], d_ss.at[1], d_rs.at[2], (d, to))

    landed(rows.at[pl.ds(0, 8)], t_rs.at[1])
    mine = rows[place]
    all_rows = rows[...].reshape(GROUP * 32, 4 * LANES)
    query_feat = lax.dot_general(
        pick[...], all_rows, (((0,), (0,)), ((), ())), preferred_element_type=jnp.float32
    ).astype(jnp.bfloat16)
    partial_scores = lax.dot_general(
        query_feat, mine, (((1,), (1,)), ((), ())), preferred_element_type=jnp.float32
    )
    for k in range(GROUP):
        score_out[8 * k : 8 * k + 4, 0:32] = partial_scores[4 * k : 4 * k + 4, :]
    for k in range(1, GROUP):
        to = lax.rem(t + k, GROUP)
        send(score_out.at[tile(to)], score_got.at[tile(t)], s_ss.at[0], s_rs.at[0], (d, to))
    score_got[tile(t), :] = score_out[tile(t), :]
    turned[...] = lax.dot_general(
        all_rows, swap[...], (((0,), (0,)), ((), ())), preferred_element_type=jnp.float32
    ).astype(jnp.bfloat16)

    landed(cols.at[pl.ds(0, 5)], d_rs.at[1])
    landed(cols.at[pl.ds(0, 6)], d_rs.at[2])
    all_cols = cols[...].reshape(GROUP * 32, 4 * LANES)
    for layer in range(2):
        span = slice(layer * 2 * LANES, (layer + 1) * 2 * LANES)
        gram[layer] = jnp.dot(
            turned[span, :], all_cols[:, span], preferred_element_type=jnp.float32
        ) * jnp.float32(1.0 / 512)

    landed(score_got.at[pl.ds(0, 8 * (GROUP - 1))], s_rs.at[0])
    total = score_got[0:8, :]
    for k in range(1, GROUP):
        total = total + score_got[8 * k : 8 * k + 8, :]
    scores[...] = total[0:4, 0:32] / jnp.float32(math.sqrt(2 * RANK * RANK))

    tiles = pl.ds(0, 8 * (GROUP - 1))
    for ref, sem in (
        (a_out, a_ss.at[0]),
        (b_out, b_ss.at[0]),
        (x_out, x_ss.at[0]),
        (land_t.at[tiles], lt_ss.at[0]),
        (land_d.at[tiles], ld_ss.at[0]),
        (rows.at[pl.ds(0, 7)], t_ss.at[0]),
        (rows.at[pl.ds(0, 8)], t_ss.at[1]),
        (cols.at[pl.ds(0, 9)], d_ss.at[0]),
        (cols.at[pl.ds(0, 6)], d_ss.at[1]),
        (score_got.at[tiles], s_ss.at[0]),
    ):
        landed(ref, sem)


def local(*args):
    tokens, width = args[0].shape
    query = args[-1].reshape(1, -1)
    dma = pltpu.SemaphoreType.DMA
    f32, bf16, i16 = jnp.float32, jnp.bfloat16, jnp.int16
    vmem = pltpu.VMEM
    scratch = [
        vmem((4, width, tokens), bf16),
        vmem((4, RANK, width), bf16),
        vmem(query.shape, jnp.int32),
        vmem((tokens // SEQ, 2, LANES, SEQ), f32),
        vmem((7, 2, PACK, LANES), i16),
        vmem((7, 2, PACK, LANES), i16),
        vmem((7, PACK, LANES), i16),
        vmem((7, PACK, LANES), i16),
        vmem((RING + 1, PACK, LANES), i16),
        vmem((RING + 1, PACK, LANES), i16),
        vmem((RANK, LANES), f32),
        vmem((8 * GROUP, LANES), f32),
        vmem((8 * GROUP, LANES), f32),
        vmem((8 * GROUP, LANES), f32),
        vmem((GROUP, 32, 4 * LANES), bf16),
        vmem((GROUP, 32, 4 * LANES), bf16),
        vmem((GROUP * 32, GROUP * 32), bf16),
        vmem((GROUP * 32, query.shape[1]), bf16),
        vmem((4 * LANES, GROUP * 32), bf16),
        vmem((8 * GROUP, LANES), f32),
        vmem((8 * GROUP, LANES), f32),
        dma((RING, 2)), dma((1,)), dma((1,)),
        dma((1,)), dma((7, 2)),
        dma((1,)), dma((7,)),
        dma((1,)), dma((RING + 1,)),
        dma((1,)), dma((1,)),
        dma((1,)), dma((1,)),
        dma((2,)), dma((2,)),
        dma((2,)), dma((3,)),
        dma((1,)), dma((1,)),
    ]
    in_hbm = pl.BlockSpec(memory_space=pltpu.HBM)
    in_vmem = pl.BlockSpec(memory_space=pltpu.VMEM)
    return pl.pallas_call(
        kernel,
        out_shape=(
            jax.ShapeDtypeStruct((2, 256, 256), f32),
            jax.ShapeDtypeStruct((4, 32), f32),
        ),
        in_specs=[in_hbm] * 9,
        out_specs=(in_vmem, in_vmem),
        scratch_shapes=scratch,
        compiler_params=pltpu.CompilerParams(
            collective_id=0, has_side_effects=True, vmem_limit_bytes=58 << 20
        ),
    )(*[arg.T for arg in args[:-1]], query)


def solution(mesh):
    in_specs = (
        P("dp", "tensor"),
        P("dp", "tensor"),
        P("dp", "tensor"),
        P("dp", "tensor"),
        P("tensor", None),
        P("tensor", None),
        P("tensor", None),
        P("tensor", None),
        P(),
    )
    out_specs = (P(None, "tensor", "dp"), P("tensor", "dp"))
    return jax.shard_map(local, mesh=mesh, in_specs=in_specs, out_specs=out_specs, check_vma=False)
```

time: 88.9 us -> 62.4 us (0.70)
  the two profiles are of different devices: /device:TPU:2 before, /device:TPU:1 now
where the time goes in v3:
time: 62.4 us; the launch traced here: 62.2 us
  Pallas kernels  58.5 us (94%)
  local copies, waits for them, and re-layouts  3.12 us (5%)
  between operations  0.64 us (1%)
    pallas_call x1, Pallas kernels, local(): pl.pallas_call(kernel, out_shape=(jax.ShapeDtypeStruct((2, 256, 256), f32...  58.5 us
    unnamed x2, local copies, waits for them, and re-layouts  3.12 us

profile of v3, /device:TPU:1, one launch (start us, length us, event | category | flops | bytes accessed | tf_op | source)
XLA Modules:
  0.0 62.2 jit_solution(8636592643776583446)
XLA Ops:
  0.6 58.5 %shard_map.104 = (f32[2,256,256]{2,1,0:T(8,128)}, f32[4,32]{1,0:T(4,128)}) custom-call(bf16[320,4096]{1,0:T(8,128)(2,1)} %bitcast.9, bf16[320,4096]{1,0:T(8,128)(2,1)} %bitcast.10, bf16[320,4096]{1,0:T(8,128)(2,1)} %bitcast.11, bf16[320,4096]{1,0:T(8,128)(2,1)} %bitcast.12, bf16[64,320]{1,0:T(8,128)(2,1)} %bitcast.13, bf16[64,320]{1,0:T(8,128)(2,1)} %bitcast.14, ...), custom_call_target="tpu_custom_call" | custom-call | tf_op jit(solution)/shard_map/pallas_call | solution.py:345
  59.1 1.9 %copy.13 = f32[2,256,256]{2,1,0:T(8,128)} copy(f32[2,256,256]{2,1,0:T(8,128)} %get-tuple-element.4) | data formatting | bytes 1048576
  61.0 1.3 %copy.14 = f32[4,32]{1,0:T(4,128)} copy(f32[4,32]{1,0:T(4,128)} %get-tuple-element.5) | data formatting | bytes 1024

commit v4 on v3

--- a/solution.py
+++ b/solution.py
@@ -72,29 +72,35 @@
     def landed(ref, sem):
         pltpu.make_async_copy(ref, ref, sem).wait()
 
+    def along(steps):
+        return lax.rem(z + steps + RING, RING)
+
     barrier = pltpu.get_barrier_semaphore()
-    for k in range(1, GROUP):
-        pl.semaphore_signal(
-            barrier, inc=1, device_id=(d, lax.rem(t + k, GROUP)), device_id_type=MESH
-        )
-        pl.semaphore_signal(
-            barrier, inc=1, device_id=(lax.rem(d + k, GROUP), t), device_id_type=MESH
-        )
-
-    def load(i):
-        for half in range(2):
-            start = pl.multiple_of((half * GROUP + 2 * owners[i]) * SEQ, 2 * SEQ)
-            for k, source in enumerate((in_one, grad_one, in_two, grad_two)):
-                pltpu.make_async_copy(
-                    source.at[:, pl.ds(start, 2 * SEQ)],
-                    tok.at[k, :, pl.ds(start, 2 * SEQ)],
-                    in_sem.at[i, half],
-                ).start()
-
+    near = [(d, along(way * steps) * 2 + side) for steps in (1, -1) for side in range(2)]
+    near += [partner] + [(lax.rem(d + k, GROUP), t) for k in range(1, GROUP)]
+
+    def greet(devices):
+        for device in devices:
+            pl.semaphore_signal(barrier, inc=1, device_id=device, device_id_type=MESH)
+
+    def load(i, half):
+        start = pl.multiple_of((half * GROUP + 2 * owners[i]) * SEQ, 2 * SEQ)
+        for k, source in enumerate((in_one, grad_one, in_two, grad_two)):
+            pltpu.make_async_copy(
+                source.at[:, pl.ds(start, 2 * SEQ)],
+                tok.at[k, :, pl.ds(start, 2 * SEQ)],
+                in_sem.at[i, half],
+            ).start()
+
+    greet(near[:5])
     for k, weight in enumerate((w_in_one, w_out_one, w_in_two, w_out_two)):
         pltpu.make_async_copy(weight, weights.at[k], w_sem.at[0]).start()
-    for i in range(3):
-        load(i)
+    load(0, 1)
+    load(0, 0)
+    greet(near[5:])
+    for i in (1, 2):
+        load(i, 1)
+        load(i, 0)
     pltpu.make_async_copy(asked, query, q_sem.at[0]).start()
     landed(weights, w_sem.at[0])
 
@@ -123,10 +129,10 @@
                 landed(a_got.at[i - 2, side], a_rs.at[i - 2, side])
                 total = add(total, decode(a_got.at[i - 2, side]))
             encode(a_out.at[i, side], total)
-            send(
-                a_out.at[i, side], a_got.at[i, side], a_ss.at[0], a_rs.at[i, side],
-                forward if i % 2 == 0 else backward,
-            )
+            lane, to = side, forward if i % 2 == 0 else backward
+            if i >= 5:
+                lane, to = xh, (d, along(way if i % 2 == 0 else -way) * 2 + side)
+            send(a_out.at[i, side], a_got.at[i, lane], a_ss.at[0], a_rs.at[i, lane], to)
 
     def pair(i):
         encode(x_out.at[i], own(1, owners[i], 1 - xh))
@@ -143,42 +149,42 @@
             b_out.at[i], b_got.at[i], b_ss.at[0], b_rs.at[i], forward if i % 2 == 0 else backward
         )
 
+    def constants():
+        at_row = lax.broadcasted_iota(jnp.int32, (GROUP * 32, GROUP * 32), 0)
+        at_col = lax.broadcasted_iota(jnp.int32, (GROUP * 32, GROUP * 32), 1)
+        mirrored = (at_row % 16) * 32 + (at_row // 16 % 2) * 16 + at_row // 32
+        swap[...] = jnp.where(at_col == mirrored, 1.0, 0.0).astype(jnp.bfloat16)
+        landed(query, q_sem.at[0])
+        row = lax.broadcasted_iota(jnp.int32, pick.shape, 0)
+        example = (row // 32 % 8 * 2 + row // 256) * 32 + row % 32
+        pick[...] = jnp.where(example == query[...], 1.0, 0.0).astype(jnp.bfloat16)
+        score_out[...] = jnp.zeros_like(score_out)
+
+    def first(i):
+        project(i, 1)
+        if i == 0:
+            pl.semaphore_wait(barrier, len(near))
+        pair(i)
+
+    first(0)
     for i in range(RING + 1):
         if i < RING:
+            if i + 3 < RING:
+                load(i + 3, 1)
+                load(i + 3, 0)
             project(i, 0)
-            if i + 3 < RING:
-                load(i + 3)
-            if i == 0:
-                pl.semaphore_wait(barrier, 2 * (GROUP - 1))
-            if i < RING - 1:
+            if i < 2:
                 ring_a(i)
-            project(i, 1)
-            pair(i)
+            if i + 1 < RING:
+                first(i + 1)
+            if 2 <= i < RING - 1:
+                ring_a(i)
+            if i == RING - 1:
+                encode(x_out.at[RING], own(0, z, 1 - xh))
+                send(x_out.at[RING], x_got.at[RING], x_ss.at[0], x_rs.at[RING], partner)
+                constants()
         if i >= 2:
             ring_b(i - 2)
-
-    for side in range(2):
-        for i in (5, 6):
-            landed(a_got.at[i, side], a_rs.at[i, side])
-
-    def over_z(side):
-        total = own(0, z, side)
-        for i in (5, 6):
-            total = add(total, decode(a_got.at[i, side]))
-        return total
-
-    encode(x_out.at[RING], over_z(1 - xh))
-    send(x_out.at[RING], x_got.at[RING], x_ss.at[0], x_rs.at[RING], partner)
-
-    at_row = lax.broadcasted_iota(jnp.int32, (GROUP * 32, GROUP * 32), 0)
-    at_col = lax.broadcasted_iota(jnp.int32, (GROUP * 32, GROUP * 32), 1)
-    mirrored = (at_row % 16) * 32 + (at_row // 16 % 2) * 16 + at_row // 32
-    swap[...] = jnp.where(at_col == mirrored, 1.0, 0.0).astype(jnp.bfloat16)
-    landed(query, q_sem.at[0])
-    row = lax.broadcasted_iota(jnp.int32, pick.shape, 0)
-    example = (row // 32 % 8 * 2 + row // 256) * 32 + row % 32
-    pick[...] = jnp.where(example == query[...], 1.0, 0.0).astype(jnp.bfloat16)
-    score_out[...] = jnp.zeros_like(score_out)
 
     def features(half, sums):
         for layer in range(2):
@@ -203,17 +209,19 @@
         total = add(total, decode(b_got.at[i]))
     features(1, total)
     landed(x_got.at[RING], x_rs.at[RING])
-    features(0, add(over_z(xh), decode(x_got.at[RING])))
+    total = add(own(0, z, xh), decode(x_got.at[RING]))
+    for i in (5, 6):
+        for side in range(2):
+            landed(a_got.at[i, side], a_rs.at[i, side])
+            total = add(total, decode(a_got.at[i, side]))
+    features(0, total)
 
     place = d % 2 * 8 + d // 2
-
-    def along(steps):
-        return lax.rem(z + steps + RING, RING)
 
     def tile(index):
         return pl.ds(pl.multiple_of(8 * index, 8), 8)
 
-    for k in range(1, GROUP):
+    for k in sorted(range(1, GROUP), key=lambda k: abs(k - 8)):
         to = lax.rem(t + k, GROUP)
         send(slices.at[tile(to)], land_t.at[tile(t)], lt_ss.at[0], lt_rs.at[0], (d, to))
     for k in range(1, GROUP):
@@ -235,22 +243,25 @@
         send(rows.at[place], rows.at[place], t_ss.at[0], t_rs.at[0], (lax.rem(d + 2 * k, GROUP), t))
 
     gather(land_d, cols.at[t], ld_rs)
-    for i, steps in enumerate((2, -2, 1, -1, 0)):
+    for steps in (2, 1, 0):
         for flip in range(2):
-            if steps or flip:
-                to = along(steps) * 2 + (1 - xh if flip else xh)
-                send(cols.at[t], cols.at[t], d_ss.at[0], d_rs.at[0 if i < 2 else 1], (d, to))
+            for sign in (1, -1) if steps else (1,):
+                if steps or flip:
+                    to = along(sign * steps) * 2 + (1 - xh if flip else xh)
+                    sem = flip if steps == 2 else 2
+                    send(cols.at[t], cols.at[t], d_ss.at[0], d_rs.at[sem], (d, to))
 
     landed(rows.at[pl.ds(0, 7)], t_rs.at[0])
     block = pl.ds(d % 2 * 8, 8)
     sibling = (d + 1 - 2 * (d % 2), t)
     send(rows.at[block], rows.at[block], t_ss.at[1], t_rs.at[1], sibling)
 
-    landed(cols.at[pl.ds(0, 4)], d_rs.at[0])
-    for held, steps in ((-2 * way, way), (-2 * way, 2 * way), (2 * way, -way)):
-        block = pl.ds(2 * along(held), 2)
-        to = along(steps) * 2 + xh
-        send(cols.at[block], cols.at[block], d_ss.at[1], d_rs.at[2], (d, to))
+    for flip in range(2):
+        landed(cols.at[pl.ds(0, 2)], d_rs.at[flip])
+        for held, steps in ((-2 * way, 2 * way), (-2 * way, way), (2 * way, -way)):
+            block = along(held) * 2 + (1 - xh if flip else xh)
+            to = along(steps) * 2 + xh
+            send(cols.at[block], cols.at[block], d_ss.at[1], d_rs.at[3], (d, to))
 
     landed(rows.at[pl.ds(0, 8)], t_rs.at[1])
     mine = rows[place]
@@ -263,7 +274,7 @@
     )
     for k in range(GROUP):
         score_out[8 * k : 8 * k + 4, 0:32] = partial_scores[4 * k : 4 * k + 4, :]
-    for k in range(1, GROUP):
+    for k in sorted(range(1, GROUP), key=lambda k: abs(k - 8)):
         to = lax.rem(t + k, GROUP)
         send(score_out.at[tile(to)], score_got.at[tile(t)], s_ss.at[0], s_rs.at[0], (d, to))
     score_got[tile(t), :] = score_out[tile(t), :]
@@ -271,8 +282,8 @@
         all_rows, swap[...], (((0,), (0,)), ((), ())), preferred_element_type=jnp.float32
     ).astype(jnp.bfloat16)
 
-    landed(cols.at[pl.ds(0, 5)], d_rs.at[1])
-    landed(cols.at[pl.ds(0, 6)], d_rs.at[2])
+    landed(cols.at[pl.ds(0, 5)], d_rs.at[2])
+    landed(cols.at[pl.ds(0, 6)], d_rs.at[3])
     all_cols = cols[...].reshape(GROUP * 32, 4 * LANES)
     for layer in range(2):
         span = slice(layer * 2 * LANES, (layer + 1) * 2 * LANES)
@@ -337,7 +348,7 @@
         dma((1,)), dma((1,)),
         dma((1,)), dma((1,)),
         dma((2,)), dma((2,)),
-        dma((2,)), dma((3,)),
+        dma((2,)), dma((4,)),
         dma((1,)), dma((1,)),
     ]
     in_hbm = pl.BlockSpec(memory_space=pltpu.HBM)

time: 62.4 us -> 59.1 us (0.947)
  Pallas kernels: 58.5 us -> 55.1 us
    pallas_call x1, Pallas kernels: 58.5 us -> 55.1 us  [local(): pl.pallas_call(kernel, out_shape=(jax.ShapeDtypeStruct((2, 256, 256), f32...]
where the time goes in v4:
time: 59.1 us; the launch traced here: 58.9 us
  Pallas kernels  55.1 us (93%)
  local copies, waits for them, and re-layouts  3.12 us (5%)
  between operations  0.64 us (1%)
    pallas_call x1, Pallas kernels, local(): pl.pallas_call(kernel, out_shape=(jax.ShapeDtypeStruct((2, 256, 256), f32...  55.1 us
    unnamed x2, local copies, waits for them, and re-layouts  3.12 us

profile of v4, /device:TPU:1, one launch (start us, length us, event | category | flops | bytes accessed | tf_op | source)
XLA Modules:
  0.0 58.9 jit_solution(17104716911846046755)
XLA Ops:
  0.6 55.1 %shard_map.104 = (f32[2,256,256]{2,1,0:T(8,128)}, f32[4,32]{1,0:T(4,128)}) custom-call(bf16[320,4096]{1,0:T(8,128)(2,1)} %bitcast.9, bf16[320,4096]{1,0:T(8,128)(2,1)} %bitcast.10, bf16[320,4096]{1,0:T(8,128)(2,1)} %bitcast.11, bf16[320,4096]{1,0:T(8,128)(2,1)} %bitcast.12, bf16[64,320]{1,0:T(8,128)(2,1)} %bitcast.13, bf16[64,320]{1,0:T(8,128)(2,1)} %bitcast.14, ...), custom_call_target="tpu_custom_call" | custom-call | tf_op jit(solution)/shard_map/pallas_call | solution.py:356
  55.8 1.9 %copy.13 = f32[2,256,256]{2,1,0:T(8,128)} copy(f32[2,256,256]{2,1,0:T(8,128)} %get-tuple-element.4) | data formatting | bytes 1048576
  57.7 1.3 %copy.14 = f32[4,32]{1,0:T(4,128)} copy(f32[4,32]{1,0:T(4,128)} %get-tuple-element.5) | data formatting | bytes 1024

commit v5 on v4

--- a/solution.py
+++ b/solution.py
@@ -52,9 +52,9 @@
     in_one, grad_one, in_two, grad_two, w_in_one, w_out_one, w_in_two, w_out_two, asked,
     gram, scores,
     tok, weights, query, part, a_out, a_got, b_out, b_got, x_out, x_got, square, slices, land_t, land_d,
-    rows, cols, swap, pick, turned, score_out, score_got,
+    rows, cols, swap, pick, turned, result, query_out, query_got, score_out, score_got,
     in_sem, w_sem, q_sem, a_ss, a_rs, b_ss, b_rs, x_ss, x_rs, lt_ss, lt_rs, ld_ss, ld_rs,
-    t_ss, t_rs, d_ss, d_rs, s_ss, s_rs,
+    t_ss, t_rs, d_ss, d_rs, s_ss, s_rs, qs_sem, g_sem,
 ):
     d = lax.axis_index("dp")
     t = lax.axis_index("tensor")
@@ -98,10 +98,6 @@
     load(0, 1)
     load(0, 0)
     greet(near[5:])
-    for i in (1, 2):
-        load(i, 1)
-        load(i, 0)
-    pltpu.make_async_copy(asked, query, q_sem.at[0]).start()
     landed(weights, w_sem.at[0])
 
     def project(i, half):
@@ -166,25 +162,41 @@
             pl.semaphore_wait(barrier, len(near))
         pair(i)
 
+    def loads(*which):
+        for i, half in which:
+            load(i, half)
+
     first(0)
-    for i in range(RING + 1):
-        if i < RING:
-            if i + 3 < RING:
-                load(i + 3, 1)
-                load(i + 3, 0)
-            project(i, 0)
-            if i < 2:
-                ring_a(i)
-            if i + 1 < RING:
-                first(i + 1)
-            if 2 <= i < RING - 1:
-                ring_a(i)
-            if i == RING - 1:
-                encode(x_out.at[RING], own(0, z, 1 - xh))
-                send(x_out.at[RING], x_got.at[RING], x_ss.at[0], x_rs.at[RING], partner)
-                constants()
-        if i >= 2:
-            ring_b(i - 2)
+    loads((1, 1), (1, 0), (2, 1), (3, 1))
+    project(0, 0)
+    ring_a(0)
+    loads((2, 0), (4, 1))
+    first(1)
+    project(1, 0)
+    ring_a(1)
+    loads((3, 0), (5, 1))
+    first(2)
+    loads((4, 0), (6, 1))
+    first(3)
+    loads((5, 0), (7, 1))
+    pltpu.make_async_copy(asked, query, q_sem.at[0]).start()
+    project(2, 0)
+    ring_b(0)
+    for i in range(2, RING - 1):
+        ring_a(i)
+        ring_b(i - 1)
+        if i == 2:
+            loads((6, 0), (7, 0))
+        if i + 2 < RING:
+            first(i + 2)
+        if i < RING - 2:
+            project(i + 1, 0)
+        if i == RING - 3:
+            project(RING - 1, 0)
+            encode(x_out.at[RING], own(0, z, 1 - xh))
+            send(x_out.at[RING], x_got.at[RING], x_ss.at[0], x_rs.at[RING], partner)
+    ring_b(RING - 2)
+    constants()
 
     def features(half, sums):
         for layer in range(2):
@@ -251,33 +263,42 @@
                     sem = flip if steps == 2 else 2
                     send(cols.at[t], cols.at[t], d_ss.at[0], d_rs.at[sem], (d, to))
 
-    landed(rows.at[pl.ds(0, 7)], t_rs.at[0])
-    block = pl.ds(d % 2 * 8, 8)
-    sibling = (d + 1 - 2 * (d % 2), t)
-    send(rows.at[block], rows.at[block], t_ss.at[1], t_rs.at[1], sibling)
-
-    for flip in range(2):
+    def further(flip):
         landed(cols.at[pl.ds(0, 2)], d_rs.at[flip])
         for held, steps in ((-2 * way, 2 * way), (-2 * way, way), (2 * way, -way)):
             block = along(held) * 2 + (1 - xh if flip else xh)
             to = along(steps) * 2 + xh
             send(cols.at[block], cols.at[block], d_ss.at[1], d_rs.at[3], (d, to))
 
-    landed(rows.at[pl.ds(0, 8)], t_rs.at[1])
-    mine = rows[place]
-    all_rows = rows[...].reshape(GROUP * 32, 4 * LANES)
-    query_feat = lax.dot_general(
-        pick[...], all_rows, (((0,), (0,)), ((), ())), preferred_element_type=jnp.float32
+    further(0)
+    landed(rows.at[pl.ds(0, 7)], t_rs.at[0])
+    side = d % 2
+    block = pl.ds(side * 8, 8)
+    sibling = (d + 1 - 2 * side, t)
+    half_pick = pick[pl.ds(pl.multiple_of(side * 256, 256), 256), :]
+    half_rows = rows[block].reshape(256, 4 * LANES)
+    query_out[...] = lax.dot_general(
+        half_pick, half_rows, (((0,), (0,)), ((), ())), preferred_element_type=jnp.float32
     ).astype(jnp.bfloat16)
+    send(query_out, query_got, qs_sem.at[0], qs_sem.at[1], sibling)
+    send(rows.at[block], rows.at[block], t_ss.at[1], t_rs.at[1], sibling)
+
+    landed(query_got, qs_sem.at[1])
     partial_scores = lax.dot_general(
-        query_feat, mine, (((1,), (1,)), ((), ())), preferred_element_type=jnp.float32
+        query_out[...] + query_got[...],
+        rows[place],
+        (((1,), (1,)), ((), ())),
+        preferred_element_type=jnp.float32,
     )
     for k in range(GROUP):
         score_out[8 * k : 8 * k + 4, 0:32] = partial_scores[4 * k : 4 * k + 4, :]
     for k in sorted(range(1, GROUP), key=lambda k: abs(k - 8)):
         to = lax.rem(t + k, GROUP)
         send(score_out.at[tile(to)], score_got.at[tile(t)], s_ss.at[0], s_rs.at[0], (d, to))
+    further(1)
     score_got[tile(t), :] = score_out[tile(t), :]
+    landed(rows.at[pl.ds(0, 8)], t_rs.at[1])
+    all_rows = rows[...].reshape(GROUP * 32, 4 * LANES)
     turned[...] = lax.dot_general(
         all_rows, swap[...], (((0,), (0,)), ((), ())), preferred_element_type=jnp.float32
     ).astype(jnp.bfloat16)
@@ -287,9 +308,10 @@
     all_cols = cols[...].reshape(GROUP * 32, 4 * LANES)
     for layer in range(2):
         span = slice(layer * 2 * LANES, (layer + 1) * 2 * LANES)
-        gram[layer] = jnp.dot(
+        result[layer] = jnp.dot(
             turned[span, :], all_cols[:, span], preferred_element_type=jnp.float32
         ) * jnp.float32(1.0 / 512)
+        pltpu.make_async_copy(result.at[layer], gram.at[layer], g_sem.at[layer]).start()
 
     landed(score_got.at[pl.ds(0, 8 * (GROUP - 1))], s_rs.at[0])
     total = score_got[0:8, :]
@@ -309,6 +331,9 @@
         (cols.at[pl.ds(0, 9)], d_ss.at[0]),
         (cols.at[pl.ds(0, 6)], d_ss.at[1]),
         (score_got.at[tiles], s_ss.at[0]),
+        (query_out, qs_sem.at[0]),
+        (result.at[0], g_sem.at[0]),
+        (result.at[1], g_sem.at[1]),
     ):
         landed(ref, sem)
 
@@ -339,6 +364,9 @@
         vmem((GROUP * 32, GROUP * 32), bf16),
         vmem((GROUP * 32, query.shape[1]), bf16),
         vmem((4 * LANES, GROUP * 32), bf16),
+        vmem((2, 256, 256), f32),
+        vmem((query.shape[1], 4 * LANES), bf16),
+        vmem((query.shape[1], 4 * LANES), bf16),
         vmem((8 * GROUP, LANES), f32),
         vmem((8 * GROUP, LANES), f32),
         dma((RING, 2)), dma((1,)), dma((1,)),
@@ -350,6 +378,7 @@
         dma((2,)), dma((2,)),
         dma((2,)), dma((4,)),
         dma((1,)), dma((1,)),
+        dma((2,)), dma((2,)),
     ]
     in_hbm = pl.BlockSpec(memory_space=pltpu.HBM)
     in_vmem = pl.BlockSpec(memory_space=pltpu.VMEM)
@@ -360,7 +389,7 @@
             jax.ShapeDtypeStruct((4, 32), f32),
         ),
         in_specs=[in_hbm] * 9,
-        out_specs=(in_vmem, in_vmem),
+        out_specs=(in_hbm, in_vmem),
         scratch_shapes=scratch,
         compiler_params=pltpu.CompilerParams(
             collective_id=0, has_side_effects=True, vmem_limit_bytes=58 << 20

time: 59.1 us -> 57.1 us (0.966)
  Pallas kernels: 55.1 us -> 53.2 us
    pallas_call x1, Pallas kernels: 55.1 us -> 53.2 us  [local(): pl.pallas_call(kernel, out_shape=(jax.ShapeDtypeStruct((2, 256, 256), f32...]
where the time goes in v5:
time: 57.1 us; the launch traced here: 57 us
  Pallas kernels  53.2 us (93%)
  local copies, waits for them, and re-layouts  3.12 us (5%)
  between operations  0.64 us (1%)
    pallas_call x1, Pallas kernels, local(): pl.pallas_call(kernel, out_shape=(jax.ShapeDtypeStruct((2, 256, 256), f32...  53.2 us
    unnamed x2, local copies, waits for them, and re-layouts  3.12 us

profile of v5, /device:TPU:1, one launch (start us, length us, event | category | flops | bytes accessed | tf_op | source)
XLA Modules:
  0.0 57.0 jit_solution(18185306591821008924)
XLA Ops:
  0.6 53.2 %shard_map.104 = (f32[2,256,256]{2,1,0:T(8,128)}, f32[4,32]{1,0:T(4,128)}) custom-call(bf16[320,4096]{1,0:T(8,128)(2,1)} %bitcast.9, bf16[320,4096]{1,0:T(8,128)(2,1)} %bitcast.10, bf16[320,4096]{1,0:T(8,128)(2,1)} %bitcast.11, bf16[320,4096]{1,0:T(8,128)(2,1)} %bitcast.12, bf16[64,320]{1,0:T(8,128)(2,1)} %bitcast.13, bf16[64,320]{1,0:T(8,128)(2,1)} %bitcast.14, ...), custom_call_target="tpu_custom_call" | custom-call | tf_op jit(solution)/shard_map/pallas_call | solution.py:385
  53.8 1.9 %copy.13 = f32[2,256,256]{2,1,0:T(8,128)} copy(f32[2,256,256]{2,1,0:T(8,128)} %get-tuple-element.4) | data formatting | bytes 1048576
  55.7 1.3 %copy.14 = f32[4,32]{1,0:T(4,128)} copy(f32[4,32]{1,0:T(4,128)} %get-tuple-element.5) | data formatting | bytes 1024

commit v6 on v5

--- a/solution.py
+++ b/solution.py
@@ -95,8 +95,8 @@
     greet(near[:5])
     for k, weight in enumerate((w_in_one, w_out_one, w_in_two, w_out_two)):
         pltpu.make_async_copy(weight, weights.at[k], w_sem.at[0]).start()
+    load(0, 0)
     load(0, 1)
-    load(0, 0)
     greet(near[5:])
     landed(weights, w_sem.at[0])
 
@@ -151,25 +151,24 @@
         mirrored = (at_row % 16) * 32 + (at_row // 16 % 2) * 16 + at_row // 32
         swap[...] = jnp.where(at_col == mirrored, 1.0, 0.0).astype(jnp.bfloat16)
         landed(query, q_sem.at[0])
-        row = lax.broadcasted_iota(jnp.int32, pick.shape, 0)
+        row = lax.broadcasted_iota(jnp.int32, pick.shape[::-1], 0)
         example = (row // 32 % 8 * 2 + row // 256) * 32 + row % 32
-        pick[...] = jnp.where(example == query[...], 1.0, 0.0).astype(jnp.bfloat16)
+        pick[...] = jnp.where(example == query[...], 1.0, 0.0).T.astype(jnp.bfloat16)
         score_out[...] = jnp.zeros_like(score_out)
 
     def first(i):
         project(i, 1)
-        if i == 0:
-            pl.semaphore_wait(barrier, len(near))
         pair(i)
 
     def loads(*which):
         for i, half in which:
             load(i, half)
 
+    project(0, 0)
+    pl.semaphore_wait(barrier, len(near))
+    ring_a(0)
     first(0)
-    loads((1, 1), (1, 0), (2, 1), (3, 1))
-    project(0, 0)
-    ring_a(0)
+    loads((1, 0), (1, 1), (2, 1), (3, 1))
     loads((2, 0), (4, 1))
     first(1)
     project(1, 0)
@@ -201,14 +200,15 @@
     def features(half, sums):
         for layer in range(2):
             outer = lax.dot_general(
-                sums[layer], sums[layer], (((1,), (1,)), ((), ())),
+                sums[layer][RANK:], sums[layer], (((1,), (1,)), ((), ())),
                 precision=lax.Precision.HIGHEST, preferred_element_type=jnp.float32,
             )
-            scaled = outer[RANK:, :] / jnp.float32(math.sqrt(SEQ))
-            square[...] = scaled.astype(jnp.bfloat16).astype(jnp.float32)
+            scaled = outer / jnp.float32(math.sqrt(SEQ))
+            square[layer] = scaled.astype(jnp.bfloat16).astype(jnp.float32)
+        for layer in range(2):
             for pair_of in range(2):
-                even = square[pl.ds(2 * pair_of, GROUP, stride=4), :]
-                odd = square[pl.ds(2 * pair_of + 1, GROUP, stride=4), :]
+                even = square[layer, pl.ds(2 * pair_of, GROUP, stride=4), :]
+                odd = square[layer, pl.ds(2 * pair_of + 1, GROUP, stride=4), :]
                 slices[pl.ds(half * 4 + layer * 2 + pair_of, GROUP, stride=8), :] = jnp.concatenate(
                     [even[:, :RANK], odd[:, :RANK]], 1
                 )
@@ -255,8 +255,8 @@
         send(rows.at[place], rows.at[place], t_ss.at[0], t_rs.at[0], (lax.rem(d + 2 * k, GROUP), t))
 
     gather(land_d, cols.at[t], ld_rs)
-    for steps in (2, 1, 0):
-        for flip in range(2):
+    for flip in range(2):
+        for steps in (2, 1, 0):
             for sign in (1, -1) if steps else (1,):
                 if steps or flip:
                     to = along(sign * steps) * 2 + (1 - xh if flip else xh)
@@ -275,10 +275,10 @@
     side = d % 2
     block = pl.ds(side * 8, 8)
     sibling = (d + 1 - 2 * side, t)
-    half_pick = pick[pl.ds(pl.multiple_of(side * 256, 256), 256), :]
+    half_pick = pick[:, pl.ds(pl.multiple_of(side * 256, 256), 256)]
     half_rows = rows[block].reshape(256, 4 * LANES)
     query_out[...] = lax.dot_general(
-        half_pick, half_rows, (((0,), (0,)), ((), ())), preferred_element_type=jnp.float32
+        half_pick, half_rows, (((1,), (0,)), ((), ())), preferred_element_type=jnp.float32
     ).astype(jnp.bfloat16)
     send(query_out, query_got, qs_sem.at[0], qs_sem.at[1], sibling)
     send(rows.at[block], rows.at[block], t_ss.at[1], t_rs.at[1], sibling)
@@ -355,14 +355,14 @@
         vmem((7, PACK, LANES), i16),
         vmem((RING + 1, PACK, LANES), i16),
         vmem((RING + 1, PACK, LANES), i16),
-        vmem((RANK, LANES), f32),
+        vmem((2, RANK, LANES), f32),
         vmem((8 * GROUP, LANES), f32),
         vmem((8 * GROUP, LANES), f32),
         vmem((8 * GROUP, LANES), f32),
         vmem((GROUP, 32, 4 * LANES), bf16),
         vmem((GROUP, 32, 4 * LANES), bf16),
         vmem((GROUP * 32, GROUP * 32), bf16),
-        vmem((GROUP * 32, query.shape[1]), bf16),
+        vmem((query.shape[1], GROUP * 32), bf16),
         vmem((4 * LANES, GROUP * 32), bf16),
         vmem((2, 256, 256), f32),
         vmem((query.shape[1], 4 * LANES), bf16),

time: 57.1 us -> 56.9 us (level)
  no operation moved by 1% of the time
where the time goes in v6:
time: 56.9 us; the launch traced here: 56.7 us
  Pallas kernels  53 us (93%)
  local copies, waits for them, and re-layouts  3.12 us (5%)
  between operations  0.64 us (1%)
    pallas_call x1, Pallas kernels, local(): pl.pallas_call(kernel, out_shape=(jax.ShapeDtypeStruct((2, 256, 256), f32...  53 us
    unnamed x2, local copies, waits for them, and re-layouts  3.12 us

profile of v6, /device:TPU:1, one launch (start us, length us, event | category | flops | bytes accessed | tf_op | source)
XLA Modules:
  0.0 56.7 jit_solution(6744331561142999119)
XLA Ops:
  0.6 53.0 %shard_map.104 = (f32[2,256,256]{2,1,0:T(8,128)}, f32[4,32]{1,0:T(4,128)}) custom-call(bf16[320,4096]{1,0:T(8,128)(2,1)} %bitcast.9, bf16[320,4096]{1,0:T(8,128)(2,1)} %bitcast.10, bf16[320,4096]{1,0:T(8,128)(2,1)} %bitcast.11, bf16[320,4096]{1,0:T(8,128)(2,1)} %bitcast.12, bf16[64,320]{1,0:T(8,128)(2,1)} %bitcast.13, bf16[64,320]{1,0:T(8,128)(2,1)} %bitcast.14, ...), custom_call_target="tpu_custom_call" | custom-call | tf_op jit(solution)/shard_map/pallas_call | solution.py:385
  53.6 1.9 %copy.13 = f32[2,256,256]{2,1,0:T(8,128)} copy(f32[2,256,256]{2,1,0:T(8,128)} %get-tuple-element.4) | data formatting | bytes 1048576
  55.5 1.3 %copy.14 = f32[4,32]{1,0:T(4,128)} copy(f32[4,32]{1,0:T(4,128)} %get-tuple-element.5) | data formatting | bytes 1024

commit v7 on v6

--- a/solution.py
+++ b/solution.py
@@ -119,7 +119,7 @@
         return [part[index, 0], part[index, 1]]
 
     def ring_a(i):
-        for side in range(2):
+        for side in (1 - xh, xh):
             total = own(0, owners[i], side)
             if i >= 2:
                 landed(a_got.at[i - 2, side], a_rs.at[i - 2, side])

time: 56.9 us -> 57.4 us (level)
  no operation moved by 1% of the time
where the time goes in v7:
time: 57.4 us; the launch traced here: 57.3 us
  Pallas kernels  53.5 us (93%)
  local copies, waits for them, and re-layouts  3.12 us (5%)
  between operations  0.64 us (1%)
    pallas_call x1, Pallas kernels, local(): pl.pallas_call(kernel, out_shape=(jax.ShapeDtypeStruct((2, 256, 256), f32...  53.5 us
    unnamed x2, local copies, waits for them, and re-layouts  3.12 us

profile of v7, /device:TPU:1, one launch (start us, length us, event | category | flops | bytes accessed | tf_op | source)
XLA Modules:
  0.0 57.3 jit_solution(107556020860119041)
XLA Ops:
  0.6 53.5 %shard_map.104 = (f32[2,256,256]{2,1,0:T(8,128)}, f32[4,32]{1,0:T(4,128)}) custom-call(bf16[320,4096]{1,0:T(8,128)(2,1)} %bitcast.9, bf16[320,4096]{1,0:T(8,128)(2,1)} %bitcast.10, bf16[320,4096]{1,0:T(8,128)(2,1)} %bitcast.11, bf16[320,4096]{1,0:T(8,128)(2,1)} %bitcast.12, bf16[64,320]{1,0:T(8,128)(2,1)} %bitcast.13, bf16[64,320]{1,0:T(8,128)(2,1)} %bitcast.14, ...), custom_call_target="tpu_custom_call" | custom-call | tf_op jit(solution)/shard_map/pallas_call | solution.py:385
  54.1 1.9 %copy.13 = f32[2,256,256]{2,1,0:T(8,128)} copy(f32[2,256,256]{2,1,0:T(8,128)} %get-tuple-element.4) | data formatting | bytes 1048576
  56.0 1.3 %copy.14 = f32[4,32]{1,0:T(4,128)} copy(f32[4,32]{1,0:T(4,128)} %get-tuple-element.5) | data formatting | bytes 1024

commit v8 on v6

--- a/solution.py
+++ b/solution.py
@@ -213,6 +213,13 @@
                     [even[:, :RANK], odd[:, :RANK]], 1
                 )
 
+    landed(x_got.at[RING], x_rs.at[RING])
+    total = add(own(0, z, xh), decode(x_got.at[RING]))
+    for i in (5, 6):
+        for side in range(2):
+            landed(a_got.at[i, side], a_rs.at[i, side])
+            total = add(total, decode(a_got.at[i, side]))
+    features(0, total)
     for i in (5, 6):
         landed(b_got.at[i], b_rs.at[i])
     landed(x_got.at[RING - 1], x_rs.at[RING - 1])
@@ -220,13 +227,6 @@
     for i in (5, 6):
         total = add(total, decode(b_got.at[i]))
     features(1, total)
-    landed(x_got.at[RING], x_rs.at[RING])
-    total = add(own(0, z, xh), decode(x_got.at[RING]))
-    for i in (5, 6):
-        for side in range(2):
-            landed(a_got.at[i, side], a_rs.at[i, side])
-            total = add(total, decode(a_got.at[i, side]))
-    features(0, total)
 
     place = d % 2 * 8 + d // 2
 

time: 56.9 us -> 57.8 us (1.016)
  Pallas kernels: 53 us -> 53.8 us
    pallas_call x1, Pallas kernels: 53 us -> 53.8 us  [local(): pl.pallas_call(kernel, out_shape=(jax.ShapeDtypeStruct((2, 256, 256), f32...]
where the time goes in v8:
time: 57.8 us; the launch traced here: 57.6 us
  Pallas kernels  53.8 us (93%)
  local copies, waits for them, and re-layouts  3.12 us (5%)
  between operations  0.64 us (1%)
    pallas_call x1, Pallas kernels, local(): pl.pallas_call(kernel, out_shape=(jax.ShapeDtypeStruct((2, 256, 256), f32...  53.8 us
    unnamed x2, local copies, waits for them, and re-layouts  3.12 us

profile of v8, /device:TPU:1, one launch (start us, length us, event | category | flops | bytes accessed | tf_op | source)
XLA Modules:
  0.0 57.6 jit_solution(2014435442118814345)
XLA Ops:
  0.6 53.8 %shard_map.104 = (f32[2,256,256]{2,1,0:T(8,128)}, f32[4,32]{1,0:T(4,128)}) custom-call(bf16[320,4096]{1,0:T(8,128)(2,1)} %bitcast.9, bf16[320,4096]{1,0:T(8,128)(2,1)} %bitcast.10, bf16[320,4096]{1,0:T(8,128)(2,1)} %bitcast.11, bf16[320,4096]{1,0:T(8,128)(2,1)} %bitcast.12, bf16[64,320]{1,0:T(8,128)(2,1)} %bitcast.13, bf16[64,320]{1,0:T(8,128)(2,1)} %bitcast.14, ...), custom_call_target="tpu_custom_call" | custom-call | tf_op jit(solution)/shard_map/pallas_call | solution.py:385
  54.5 1.9 %copy.13 = f32[2,256,256]{2,1,0:T(8,128)} copy(f32[2,256,256]{2,1,0:T(8,128)} %get-tuple-element.4) | data formatting | bytes 1048576
  56.4 1.3 %copy.14 = f32[4,32]{1,0:T(4,128)} copy(f32[4,32]{1,0:T(4,128)} %get-tuple-element.5) | data formatting | bytes 1024
